TPU v7x, 32 devices: a whole 2x2x4 slice. The times are simulated.
32 devices in a mesh: span: 8 (over z, x), ctx: 4 (over y, core).
Axes of the slice: x: 2, y: 2, z: 4, core: 2. Of those that a mesh axis runs over, the one named last changes fastest.
Arguments:
- queries: bfloat16 [4096, 3072], P(('span', 'ctx')), may hold values from -64 to 64
- keys: bfloat16 [4096, 512], P(('span', 'ctx')), may hold values from -16 to 16
- values: bfloat16 [4096, 512], P(('span', 'ctx')), may hold values from -6 to 6
- temps: float32 [8, 24], replicated, may hold values from 0.5 to 2
- levels: int32 [8], replicated, may hold values from 0 to 7
- ctx_list: int32 [8, 4], replicated, may hold values from -1 to 6, as said below
- counts: int32 [8], replicated, may hold values from 256 to 512
Outputs:
- attended: bfloat16 [4096, 3072], P(('span', 'ctx'))
Inputs may be any that keep to these rules, and one draw needn't show every extreme that they name: `ctx_list`: slot 0 of span c's list is c - 1 (-1 for span 0). Slot 1, when used, is span 0. The other slots hold distinct spans below c - 1, used slots first, then -1. The list of span 8 - 1 has no -1.
All inputs are finite; a program needn't handle non-finite values.
Results may differ from a plain program's by a relative error of at most 0.0041.
Values may be sent and summed in bfloat16 or wider, within the bound.
No kernel may reach another device: no remote copies, remote signals or barrier semaphores. Data moves between devices by JAX's collectives and lax.ppermute only.
A program may use at most 128 MiB of HBM per device.

v0:
```python
import functools
import math

import jax
import jax.numpy as jnp
from jax import lax
from jax.experimental import pallas as pl
from jax.experimental.pallas import tpu as pltpu
from jax.sharding import PartitionSpec as P

HQ = 24
KVH = 4
HD = 128
GROUP = HQ // KVH
WIDE = GROUP * HD
LOW = -1e30
SCALE = math.log2(math.e) / math.sqrt(HD)
SMEM = pl.BlockSpec(memory_space=pltpu.SMEM)
VMEM = pl.BlockSpec(memory_space=pltpu.VMEM)
PARAMS = pltpu.CompilerParams(vmem_limit_bytes=32 << 20)


def attend_kernel(backs, blocks, first, final, where_ref, levels_ref, temps_ref, list_ref, counts_ref, q_ref, *refs):
    refs = list(refs)
    if not first:
        del refs[:2]
    slabs = [(refs.pop(0), refs.pop(0)) for _ in backs]
    out_ref = refs.pop(0) if final else None
    sums_ref, top_ref, key_ref, value_ref = refs
    base = where_ref[0] & -2
    core = where_ref[1] & 1
    head = 2 * (where_ref[0] & 1) + (where_ref[1] >> 1)
    span_rows = q_ref.shape[0] // 2
    piece = span_rows // 4
    part = piece // 2
    half = slabs[0][0].shape[0] // 2
    group = GROUP // 2
    chains = [(block, g) for block in blocks for g in range(2)]

    if first:
        sums_ref[...] = jnp.zeros_like(sums_ref)
        top_ref[...] = jnp.full_like(top_ref, LOW)

    def wanted(span, ident):
        found = span == ident
        for j in range(list_ref.shape[1]):
            found = found | (list_ref[span, j] == ident)
        return found & (ident >= 0)

    index = lax.broadcasted_iota(jnp.int32, (half, HD), 0)
    for slab, back in zip(slabs, backs):
        for x in range(2):
            count = counts_ref[jnp.maximum(base + x - 2 * back, 0)]
            spare = slab[0][x * half : x * half + 16, :HD].astype(jnp.float32)[0:1]
            for side, ref in enumerate(slab):
                token = (index // piece) * (2 * piece) + (core ^ side) * piece + index % piece
                keep = token < count
                at = slice(x * half, (x + 1) * half)
                to = slice(side * half, (side + 1) * half)
                keys = jnp.where(keep, ref[at, :HD].astype(jnp.float32), spare)
                values = jnp.where(keep, ref[at, HD:].astype(jnp.float32), 0.0)
                key_ref[x, :, to] = jnp.transpose(keys).astype(jnp.bfloat16)
                value_ref[x, to, :HD] = values.astype(jnp.bfloat16)
                value_ref[x, to, HD:] = jnp.where(keep, 1.0, 0.0).astype(jnp.bfloat16)

        @pl.loop(0, 4)
        def _(turn):
            side = turn >> 1
            x = turn & 1
            span = base + side

            @pl.when(wanted(span, base + x - 2 * back))
            def _():
                level = levels_ref[span]
                keys = key_ref[x]
                values = value_ref[x]

                def scores(block, g):
                    rows = []
                    for i in range(group):
                        lanes = slice((g * group + i) * HD, (g * group + i + 1) * HD)
                        for t in range(4):
                            at = pl.multiple_of(side * span_rows + t * piece + block * part, part)
                            rows.append(q_ref[pl.ds(at, part), lanes])
                    return jnp.dot(jnp.concatenate(rows, axis=0), keys, preferred_element_type=jnp.float32)

                ready = scores(*chains[0])
                for n, (block, g) in enumerate(chains):
                    s = ready
                    if n + 1 < len(chains):
                        ready = scores(*chains[n + 1])
                    step = s.shape[0] // group
                    s = jnp.concatenate(
                        [
                            s[i * step : (i + 1) * step] * (temps_ref[level, head * GROUP + g * group + i] * SCALE)
                            for i in range(group)
                        ],
                        axis=0,
                    )
                    chain = 2 * block + g
                    old_top = top_ref[side, chain]
                    top = jnp.maximum(old_top, jnp.max(s, axis=1, keepdims=True))
                    weight = jnp.concatenate(
                        [jnp.exp2(s[:, at : at + HD] - top).astype(jnp.bfloat16) for at in range(0, s.shape[1], HD)],
                        axis=1,
                    )
                    sums = jnp.dot(weight, values, preferred_element_type=jnp.float32)
                    shrink = jnp.exp2(old_top - top)
                    sums_ref[side, chain] = sums + sums_ref[side, chain] * jnp.concatenate([shrink, shrink], axis=1)
                    top_ref[side, chain] = top

    if final:
        for side in range(2):
            for block, g in chains:
                sums = sums_ref[side, 2 * block + g]
                result = (sums[:, :HD] / sums[:, HD:]).astype(jnp.bfloat16)
                for i in range(group):
                    lanes = slice((g * group + i) * HD, (g * group + i + 1) * HD)
                    for t in range(4):
                        to = (4 * side + t) * part
                        at = (4 * i + t) * part
                        out_ref[to : to + part, lanes] = result[at : at + part]


def attend(scalars, q, state, slabs, backs, blocks, final):
    tall = GROUP * q.shape[0] // 8
    tokens = slabs[0][0].shape[0]
    out_shape = [
        jax.ShapeDtypeStruct((2, 4, tall, 2 * HD), jnp.float32),
        jax.ShapeDtypeStruct((2, 4, tall, HD), jnp.float32),
    ]
    if final:
        out_shape = [jax.ShapeDtypeStruct((q.shape[0] // 2, q.shape[1]), jnp.bfloat16)] + out_shape
    work = len(backs) * len(blocks) * 4 * tall * tokens
    return pl.pallas_call(
        functools.partial(attend_kernel, backs, blocks, state is None, final),
        out_shape=out_shape,
        in_specs=[SMEM] * 5 + [VMEM] * (1 + (0 if state is None else 2) + 2 * len(backs)),
        out_specs=[VMEM] * len(out_shape),
        scratch_shapes=[pltpu.VMEM((2, HD, tokens), jnp.bfloat16), pltpu.VMEM((2, tokens, 2 * HD), jnp.bfloat16)],
        input_output_aliases={} if state is None else {6: final + 0, 7: final + 1},
        compiler_params=PARAMS,
        cost_estimate=pl.CostEstimate(flops=4 * work * HD, bytes_accessed=2 * q.size, transcendentals=work),
    )(*scalars, q, *(state or ()), *[a for slab in slabs for a in slab])


def per_device(spans, ctx, queries, keys, values, temps, levels, ctx_list, counts):
    where = jnp.stack([lax.axis_index("span"), lax.axis_index("ctx")]).astype(jnp.int32)
    scalars = (where, levels, temps, ctx_list, counts)
    planes = [list(range(p * ctx, (p + 2) * ctx)) for p in range(0, spans, 2)]
    other_core = [(t, t ^ 1) for t in range(ctx)]
    rows = keys.shape[0]
    last = spans // 2 - 1

    def exchange(a):
        return lax.all_to_all(a, ("span", "ctx"), 0, 0, axis_index_groups=planes, tiled=True)

    def by_head(a):
        width = a.shape[1] // KVH
        a = jnp.transpose(a.reshape(2, rows // 2, KVH, width), (2, 0, 1, 3))
        return a.reshape(KVH * rows, width)

    def up(a, steps):
        return lax.ppermute(a, "span", [(s, (s + 2 * steps) % spans) for s in range(spans)])

    def near(a):
        return lax.ppermute(a, "ctx", other_core)

    own = exchange(jnp.concatenate([by_head(keys), by_head(values)], axis=1))
    slabs = {0: own, 1: up(own, 1), last: up(own, last)}
    q = exchange(by_head(queries))
    others = {back: near(slab) for back, slab in slabs.items()}
    slabs, others = lax.optimization_barrier((slabs, others))
    stage = sorted(slabs)
    state = None
    for back in range(2, last + 1):
        state = attend(scalars, q, state, [(slabs[b], others[b]) for b in stage], stage, (0, 1), False)
        if back < last:
            slabs[back] = up(slabs[back - 1], 1)
            slabs[back], state = lax.optimization_barrier((slabs[back], state))
            others[back] = near(slabs[back])
            stage = [back]
        if back >= last - 1:
            break
    result = []
    for block in range(2):
        out, *state = attend(scalars, q, state, [(slabs[b], others[b]) for b in stage], stage, (block,), True)
        result.append(exchange(out).reshape(KVH, 2, 1, rows // 4, WIDE))
    out = jnp.concatenate(result, axis=2)
    return jnp.transpose(out, (1, 2, 3, 0, 4)).reshape(rows, HQ * HD)


def solution(mesh):
    return jax.shard_map(
        functools.partial(per_device, mesh.shape["span"], mesh.shape["ctx"]),
        mesh=mesh,
        in_specs=(
            P(("span", "ctx"), None),
            P(("span", "ctx"), None),
            P(("span", "ctx"), None),
            P(),
            P(),
            P(),
            P(),
        ),
        out_specs=P(("span", "ctx"), None),
        check_vma=False,
    )
```

profile of v0, /device:TPU:25, one launch (start us, length us, event | category | flops | bytes accessed | tf_op | source)
XLA Modules:
  0.0 84.4 jit_solution(17277200159455536590)
XLA Ops:
  0.0 0.9 %reshape.37 = bf16[2,64,4,128]{3,2,1,0:T(4,128)(2,1)S(1)} reshape(bf16[128,512]{1,0:T(8,128)(2,1)} %param.8) | data formatting | bytes 262144 | tf_op jit(solution)/shard_map/reshape | solution.py:160
  1.0 0.0 copy-start.22
  1.0 0.0 copy-start.11
  1.0 0.0 copy-start.12
  1.0 0.0 copy-start.13
  1.0 1.0 %reshape.38 = bf16[2,64,4,128]{3,2,1,0:T(4,128)(2,1)S(1)} reshape(bf16[128,512]{1,0:T(8,128)(2,1)} %param.9) | data formatting | bytes 262144 | tf_op jit(solution)/shard_map/reshape | solution.py:160
  2.0 0.7 pad_maximum_fusion.1
  2.7 4.4 %all-to-all-start.1 = ((bf16[8,64,256]{2,1,0:T(8,128)(2,1)}), bf16[8,64,256]{2,1,0:T(8,128)(2,1)S(1)}, u32[]{:S(2)}, u32[]{:S(2)}) async-start(bf16[8,64,256]{2,1,0:T(8,128)(2,1)} %pad_maximum_fusion.1), calls=%async_computation.1 | async-start | bytes 524288 | tf_op jit(solution)/shard_map/all_to_all | solution.py:156
  7.1 2.0 %reshape.36 = bf16[2,64,4,768]{3,2,1,0:T(4,128)(2,1)S(1)} reshape(bf16[128,3072]{1,0:T(8,128)(2,1)} %param.7) | data formatting | bytes 1572864 | tf_op jit(solution)/shard_map/reshape | solution.py:160
  9.1 1.0 %copy.12 = bf16[4,2,64,768]{3,2,1,0:T(8,128)(2,1)} copy(bf16[4,2,64,768]{3,0,2,1:T(4,128)(2,1)S(1)} %bitcast.28) | data formatting | bytes 1572864 | tf_op jit(solution)/shard_map/transpose | solution.py:160
  10.1 2.3 %all-to-all-done.1 = bf16[8,64,256]{2,1,0:T(8,128)(2,1)S(1)} async-done(((bf16[8,64,256]{2,1,0:T(8,128)(2,1)}), bf16[8,64,256]{2,1,0:T(8,128)(2,1)S(1)}, u32[]{:S(2)}, u32[]{:S(2)}) %all-to-all-start.1) | async-done | bytes 262176 | tf_op jit(solution)/shard_map/all_to_all | solution.py:156
  12.4 4.2 %all-to-all-start = ((bf16[8,64,768]{2,1,0:T(8,128)(2,1)}), bf16[8,64,768]{2,1,0:T(8,128)(2,1)S(1)}, u32[]{:S(2)}, u32[]{:S(2)}) async-start(bf16[8,64,768]{2,1,0:T(8,128)(2,1)} %bitcast.3), calls=%async_computation | async-start | bytes 1572864 | tf_op jit(solution)/shard_map/all_to_all | solution.py:156
  16.6 0.2 collective-permute-start.1
  16.8 3.1 %collective-permute-start = (bf16[512,256]{1,0:T(8,128)(2,1)S(1)}, bf16[512,256]{1,0:T(8,128)(2,1)}, u32[]{:S(2)}, u32[]{:S(2)}) collective-permute-start(bf16[512,256]{1,0:T(8,128)(2,1)S(1)} %bitcast.24), channel_id=1, source_target_pairs={{0,8},{4,12},{8,16},{12,20},{16,24},{20,28},{24,0},{28,4},{1,9},{5... | collective-permute-start | bytes 786440 | tf_op jit(solution)/shard_map/ppermute | solution.py:164
  19.9 0.7 collective-permute-start.2
  20.6 5.6 %collective-permute-done.1.refs_4_ = bf16[512,256]{1,0:T(8,128)(2,1)S(1)} collective-permute-done((bf16[512,256]{1,0:T(8,128)(2,1)S(1)}, bf16[512,256]{1,0:T(8,128)(2,1)S(1)}, u32[]{:S(2)}, u32[]{:S(2)}) %collective-permute-start.1) | collective-permute-done | bytes 262176 | tf_op jit(solution)/shard_map/ppermute | solution.py:164
  26.3 1.5 %collective-permute-start.4 = (bf16[512,256]{1,0:T(8,128)(2,1)S(1)}, bf16[512,256]{1,0:T(8,128)(2,1)S(1)}, u32[]{:S(2)}, u32[]{:S(2)}) collective-permute-start(bf16[512,256]{1,0:T(8,128)(2,1)S(1)} %collective-permute-done.1.refs_4_), channel_id=1, source_target_pairs={{0,1},{1,0},{2,3},{3,2},{4,5},{5,4},{6,7},{7,6},{8,9},{9,8},{10,11... | collective-permute-start | bytes 786440 | tf_op jit(solution)/shard_map/ppermute | solution.py:167
  27.8 0.7 copy-done.14
  28.5 1.5 %collective-permute-done.refs_2_ = bf16[512,256]{1,0:T(8,128)(2,1)} collective-permute-done((bf16[512,256]{1,0:T(8,128)(2,1)S(1)}, bf16[512,256]{1,0:T(8,128)(2,1)}, u32[]{:S(2)}, u32[]{:S(2)}) %collective-permute-start) | collective-permute-done | bytes 262176 | tf_op jit(solution)/shard_map/ppermute | solution.py:164
  30.0 1.3 %collective-permute-start.3 = (bf16[512,256]{1,0:T(8,128)(2,1)}, bf16[512,256]{1,0:T(8,128)(2,1)S(1)}, u32[]{:S(2)}, u32[]{:S(2)}) collective-permute-start(bf16[512,256]{1,0:T(8,128)(2,1)} %collective-permute-done.refs_2_), channel_id=1, source_target_pairs={{0,1},{1,0},{2,3},{3,2},{4,5},{5,4},{6,7},{7,6},{8,9},{9,8},{10,11... | collective-permute-start | bytes 786440 | tf_op jit(solution)/shard_map/ppermute | solution.py:167
  31.3 0.0 collective-permute-done.2.refs_1_
  31.3 0.7 copy-done.16
  32.0 0.0 collective-permute-done.4.refs_5_
  32.0 0.7 copy-done.18
  32.7 0.0 collective-permute-done.3.refs_3_
  32.7 0.7 copy-done.20
  33.4 1.8 %collective-permute-start.5 = (bf16[512,256]{1,0:T(8,128)(2,1)}, bf16[512,256]{1,0:T(8,128)(2,1)S(1)}, u32[]{:S(2)}, u32[]{:S(2)}) collective-permute-start(bf16[512,256]{1,0:T(8,128)(2,1)} %collective-permute-done.refs_2_), channel_id=1, source_target_pairs={{0,8},{4,12},{8,16},{12,20},{16,24},{20,28},{24,0},{28,4},{1,9},{5... | collective-permute-start | bytes 786440 | tf_op jit(solution)/shard_map/ppermute | solution.py:164
  35.2 0.1 pad_add_fusion.where_ref
  35.3 0.0 copy-done.22
  35.3 0.1 copy.16.list_ref
  35.3 0.0 all-to-all-done
  35.3 0.0 copy-done.9
  35.3 0.9 %copy-done = bf16[8,64,768]{2,1,0:T(8,128)(2,1)} copy-done((bf16[8,64,768]{2,1,0:T(8,128)(2,1)}, bf16[8,64,768]{2,1,0:T(8,128)(2,1)S(1)}, u32[]{:S(2)}) %copy-start) | copy-done | bytes 786456
  36.2 0.0 copy-done.11
  36.2 0.0 copy-done.12
  36.2 0.0 copy-done.13
  36.2 1.1 %copy-done.1 = bf16[8,64,768]{2,1,0:T(8,128)(2,1)S(1)} copy-done((bf16[8,64,768]{2,1,0:T(8,128)(2,1)S(1)}, bf16[8,64,768]{2,1,0:T(8,128)(2,1)}, u32[]{:S(2)}) %copy-start.1) | copy-done | bytes 786456
  37.4 0.9 %copy-done.10 = bf16[8,64,256]{2,1,0:T(8,128)(2,1)S(1)} copy-done((bf16[8,64,256]{2,1,0:T(8,128)(2,1)S(1)}, bf16[8,64,256]{2,1,0:T(8,128)(2,1)}, u32[]{:S(2)}) %copy-start.10) | copy-done | bytes 262168
  38.3 0.9 %copy-done.15 = bf16[512,256]{1,0:T(8,128)(2,1)S(1)} copy-done((bf16[512,256]{1,0:T(8,128)(2,1)S(1)}, bf16[512,256]{1,0:T(8,128)(2,1)}, u32[]{:S(2)}) %copy-start.15) | copy-done | bytes 262168
  39.3 0.9 %copy-done.17 = bf16[512,256]{1,0:T(8,128)(2,1)S(1)} copy-done((bf16[512,256]{1,0:T(8,128)(2,1)S(1)}, bf16[512,256]{1,0:T(8,128)(2,1)}, u32[]{:S(2)}) %copy-start.17) | copy-done | bytes 262168
  40.2 0.9 %copy-done.19 = bf16[512,256]{1,0:T(8,128)(2,1)S(1)} copy-done((bf16[512,256]{1,0:T(8,128)(2,1)S(1)}, bf16[512,256]{1,0:T(8,128)(2,1)}, u32[]{:S(2)}) %copy-start.19) | copy-done | bytes 262168
  41.2 0.9 %copy-done.21 = bf16[512,256]{1,0:T(8,128)(2,1)S(1)} copy-done((bf16[512,256]{1,0:T(8,128)(2,1)S(1)}, bf16[512,256]{1,0:T(8,128)(2,1)}, u32[]{:S(2)}) %copy-start.21) | copy-done | bytes 262168
  42.1 12.0 %shard_map.73 = (f32[2,4,384,256]{3,2,1,0:T(8,128)S(1)}, f32[2,4,384,128]{3,2,1,0:T(8,128)S(1)}) custom-call(s32[2]{0:T(128)S(1)} %pad_add_fusion.where_ref, s32[8]{0:T(128)S(1)} %copy-done.12, f32[8,24]{1,0:T(8,128)S(1)} %copy-done.11, s32[8,4]{1,0:T(8,128)S(1)} %copy.16.list_ref, s32[8]{0:T(128)S(1)} %copy-done.13, bf16[512,768]{1,0:T(8,128)(2,1)S(1)} %bitcast.18, ...), custom_call_target="tpu_custom_call" | custom-call | flops 2415919104 | bytes 786432 | tf_op jit(solution)/shard_map/pallas_call | solution.py:135
  54.1 0.0 collective-permute-done.5.refs_2_
  54.1 0.7 collective-permute-start.6
  54.8 1.2 %collective-permute-done.6.refs_3_ = bf16[512,256]{1,0:T(8,128)(2,1)S(1)} collective-permute-done((bf16[512,256]{1,0:T(8,128)(2,1)S(1)}, bf16[512,256]{1,0:T(8,128)(2,1)S(1)}, u32[]{:S(2)}, u32[]{:S(2)}) %collective-permute-start.6) | collective-permute-done | bytes 262176 | tf_op jit(solution)/shard_map/ppermute | solution.py:167
  55.9 2.6 %shard_map.74 = (bf16[256,768]{1,0:T(8,128)(2,1)S(1)}, f32[2,4,384,256]{3,2,1,0:T(8,128)S(1)}, f32[2,4,384,128]{3,2,1,0:T(8,128)S(1)}) custom-call(s32[2]{0:T(128)S(1)} %pad_add_fusion.where_ref, s32[8]{0:T(128)S(1)} %copy-done.12, f32[8,24]{1,0:T(8,128)S(1)} %copy-done.11, s32[8,4]{1,0:T(8,128)S(1)} %copy.16.list_ref, ...), custom_call_target="tpu_custom_call", output_to_operand_aliasing={{1}: (6, {}), {2}: (7, {})} | custom-call | flops 402653184 | bytes 786432 | tf_op jit(solution)/shard_map/pallas_call | solution.py:135
  58.6 0.0 copy-done.5
  58.6 1.2 %copy-done.3 = f32[2,4,384,128]{3,2,1,0:T(8,128)} copy-done((f32[2,4,384,128]{3,2,1,0:T(8,128)}, f32[2,4,384,128]{3,2,1,0:T(8,128)S(1)}, u32[]{:S(2)}) %copy-start.3) | copy-done | bytes 1572888
  59.8 0.7 copy-done.8
  60.5 4.3 %all-to-all-start.2 = ((bf16[8,32,768]{2,1,0:T(8,128)(2,1)}), bf16[8,32,768]{2,1,0:T(8,128)(2,1)}, u32[]{:S(2)}, u32[]{:S(2)}) async-start(bf16[8,32,768]{2,1,0:T(8,128)(2,1)} %bitcast.22), calls=%async_computation.2 | async-start | bytes 786432 | tf_op jit(solution)/shard_map/all_to_all | solution.py:156
  64.9 1.1 %copy-done.2 = bf16[8,64,768]{2,1,0:T(8,128)(2,1)S(1)} copy-done((bf16[8,64,768]{2,1,0:T(8,128)(2,1)S(1)}, bf16[8,64,768]{2,1,0:T(8,128)(2,1)}, u32[]{:S(2)}) %copy-start.2) | copy-done | bytes 786456
  66.0 1.4 %copy-done.4 = f32[2,4,384,128]{3,2,1,0:T(8,128)S(1)} copy-done((f32[2,4,384,128]{3,2,1,0:T(8,128)S(1)}, f32[2,4,384,128]{3,2,1,0:T(8,128)}, u32[]{:S(2)}) %copy-start.4) | copy-done | bytes 1572888
  67.4 0.9 %copy-done.6 = bf16[512,256]{1,0:T(8,128)(2,1)S(1)} copy-done((bf16[512,256]{1,0:T(8,128)(2,1)S(1)}, bf16[512,256]{1,0:T(8,128)(2,1)}, u32[]{:S(2)}) %copy-start.6) | copy-done | bytes 262168
  68.3 2.6 %shard_map.75 = (bf16[256,768]{1,0:T(8,128)(2,1)S(1)}, f32[2,4,384,256]{3,2,1,0:T(8,128)S(1)}, f32[2,4,384,128]{3,2,1,0:T(8,128)S(1)}) custom-call(s32[2]{0:T(128)S(1)} %pad_add_fusion.where_ref, s32[8]{0:T(128)S(1)} %copy-done.12, f32[8,24]{1,0:T(8,128)S(1)} %copy-done.11, s32[8,4]{1,0:T(8,128)S(1)} %copy.16.list_ref, ...), custom_call_target="tpu_custom_call", output_to_operand_aliasing={{1}: (6, {}), {2}: (7, {})} | custom-call | flops 402653184 | bytes 786432 | tf_op jit(solution)/shard_map/pallas_call | solution.py:135
  71.0 0.0 copy-start.7
  71.0 0.7 copy-done.7
  71.7 0.0 all-to-all-done.2
  71.7 4.2 %all-to-all-start.3 = ((bf16[8,32,768]{2,1,0:T(8,128)(2,1)}), bf16[8,32,768]{2,1,0:T(8,128)(2,1)S(1)}, u32[]{:S(2)}, u32[]{:S(2)}) async-start(bf16[8,32,768]{2,1,0:T(8,128)(2,1)} %bitcast.21), calls=%async_computation.3 | async-start | bytes 786432 | tf_op jit(solution)/shard_map/all_to_all | solution.py:156
  76.0 1.3 %copy.18 = bf16[4,2,1,32,768]{4,0,3,2,1:T(4,128)(2,1)S(1)} copy(bf16[4,2,1,32,768]{4,3,1,0,2:T(8,128)(2,1)} %bitcast.11) | data formatting | bytes 786432 | tf_op jit(solution)/shard_map/reshape | solution.py:188
  77.3 5.3 %all-to-all-done.3 = bf16[8,32,768]{2,1,0:T(8,128)(2,1)S(1)} async-done(((bf16[8,32,768]{2,1,0:T(8,128)(2,1)}), bf16[8,32,768]{2,1,0:T(8,128)(2,1)S(1)}, u32[]{:S(2)}, u32[]{:S(2)}) %all-to-all-start.3) | async-done | bytes 393248 | tf_op jit(solution)/shard_map/all_to_all | solution.py:156
  82.6 0.3 copy.19
  82.9 0.6 pad_maximum_fusion
  83.4 1.0 %copy.20 = bf16[16,8,4,768]{3,1,2,0:T(8,128)(2,1)} copy(bf16[16,8,4,768]{3,2,1,0:T(4,128)(2,1)S(1)} %bitcast.27) | data formatting | bytes 1572864
  (20 shorter events, 0.1 us)
Async XLA Ops:
  1.0 34.3 %copy-start.22 = (s32[8,4]{0,1:T(4,128)S(1)}, s32[8,4]{0,1:T(4,128)}, u32[]{:S(2)}) copy-start(s32[8,4]{0,1:T(4,128)} %param.12) | copy-start | bytes 388
  1.0 35.2 %copy-start.11 = (f32[8,24]{1,0:T(8,128)S(1)}, f32[8,24]{1,0:T(8,128)}, u32[]{:S(2)}) copy-start(f32[8,24]{1,0:T(8,128)} %temps_ref.5) | copy-start | bytes 2308
  1.0 35.2 %copy-start.12 = (s32[8]{0:T(128)S(1)}, s32[8]{0:T(128)}, u32[]{:S(2)}) copy-start(s32[8]{0:T(128)} %levels_ref.5) | copy-start | bytes 100
  1.0 35.2 %copy-start.13 = (s32[8]{0:T(128)S(1)}, s32[8]{0:T(128)}, u32[]{:S(2)}) copy-start(s32[8]{0:T(128)} %counts_ref.5) | copy-start | bytes 100
  2.7 9.7 %all-to-all-start.1 = ((bf16[8,64,256]{2,1,0:T(8,128)(2,1)}), bf16[8,64,256]{2,1,0:T(8,128)(2,1)S(1)}, u32[]{:S(2)}, u32[]{:S(2)}) async-start(bf16[8,64,256]{2,1,0:T(8,128)(2,1)} %pad_maximum_fusion.1), calls=%async_computation.1 | async-start | bytes 524288 | tf_op jit(solution)/shard_map/all_to_all | solution.py:156
  12.4 22.9 %copy-start.9 = (bf16[8,64,256]{2,1,0:T(8,128)(2,1)}, bf16[8,64,256]{2,1,0:T(8,128)(2,1)S(1)}, u32[]{:S(2)}) copy-start(bf16[8,64,256]{2,1,0:T(8,128)(2,1)S(1)} %all-to-all-done.1) | copy-start | bytes 786436
  12.4 22.9 %all-to-all-start = ((bf16[8,64,768]{2,1,0:T(8,128)(2,1)}), bf16[8,64,768]{2,1,0:T(8,128)(2,1)S(1)}, u32[]{:S(2)}, u32[]{:S(2)}) async-start(bf16[8,64,768]{2,1,0:T(8,128)(2,1)} %bitcast.3), calls=%async_computation | async-start | bytes 1572864 | tf_op jit(solution)/shard_map/all_to_all | solution.py:156
  16.6 9.6 %collective-permute-start.1 = (bf16[512,256]{1,0:T(8,128)(2,1)S(1)}, bf16[512,256]{1,0:T(8,128)(2,1)S(1)}, u32[]{:S(2)}, u32[]{:S(2)}) collective-permute-start(bf16[512,256]{1,0:T(8,128)(2,1)S(1)} %bitcast.23), channel_id=1, source_target_pairs={{0,24},{4,28},{8,0},{12,4},{16,8},{20,12},{24,16},{28,20},{1,25},{... | collective-permute-start | bytes 786440 | tf_op jit(solution)/shard_map/ppermute | solution.py:164
  16.8 13.2 %collective-permute-start = (bf16[512,256]{1,0:T(8,128)(2,1)S(1)}, bf16[512,256]{1,0:T(8,128)(2,1)}, u32[]{:S(2)}, u32[]{:S(2)}) collective-permute-start(bf16[512,256]{1,0:T(8,128)(2,1)S(1)} %bitcast.24), channel_id=1, source_target_pairs={{0,8},{4,12},{8,16},{12,20},{16,24},{20,28},{24,0},{28,4},{1,9},{5... | collective-permute-start | bytes 786440 | tf_op jit(solution)/shard_map/ppermute | solution.py:164
  19.9 11.4 %collective-permute-start.2 = (bf16[512,256]{1,0:T(8,128)(2,1)S(1)}, bf16[512,256]{1,0:T(8,128)(2,1)S(1)}, u32[]{:S(2)}, u32[]{:S(2)}) collective-permute-start(bf16[512,256]{1,0:T(8,128)(2,1)S(1)} %bitcast.25), channel_id=1, source_target_pairs={{0,1},{1,0},{2,3},{3,2},{4,5},{5,4},{6,7},{7,6},{8,9},{9,8},{10,11... | collective-permute-start | bytes 786440 | tf_op jit(solution)/shard_map/ppermute | solution.py:167
  26.3 5.7 %collective-permute-start.4 = (bf16[512,256]{1,0:T(8,128)(2,1)S(1)}, bf16[512,256]{1,0:T(8,128)(2,1)S(1)}, u32[]{:S(2)}, u32[]{:S(2)}) collective-permute-start(bf16[512,256]{1,0:T(8,128)(2,1)S(1)} %collective-permute-done.1.refs_4_), channel_id=1, source_target_pairs={{0,1},{1,0},{2,3},{3,2},{4,5},{5,4},{6,7},{7,6},{8,9},{9,8},{10,11... | collective-permute-start | bytes 786440 | tf_op jit(solution)/shard_map/ppermute | solution.py:167
  27.8 0.7 copy-start.14
  30.0 2.7 %collective-permute-start.3 = (bf16[512,256]{1,0:T(8,128)(2,1)}, bf16[512,256]{1,0:T(8,128)(2,1)S(1)}, u32[]{:S(2)}, u32[]{:S(2)}) collective-permute-start(bf16[512,256]{1,0:T(8,128)(2,1)} %collective-permute-done.refs_2_), channel_id=1, source_target_pairs={{0,1},{1,0},{2,3},{3,2},{4,5},{5,4},{6,7},{7,6},{8,9},{9,8},{10,11... | collective-permute-start | bytes 786440 | tf_op jit(solution)/shard_map/ppermute | solution.py:167
  31.3 0.7 copy-start.16
  32.0 0.7 copy-start.18
  32.7 0.7 copy-start.20
  33.4 20.7 %collective-permute-start.5 = (bf16[512,256]{1,0:T(8,128)(2,1)}, bf16[512,256]{1,0:T(8,128)(2,1)S(1)}, u32[]{:S(2)}, u32[]{:S(2)}) collective-permute-start(bf16[512,256]{1,0:T(8,128)(2,1)} %collective-permute-done.refs_2_), channel_id=1, source_target_pairs={{0,8},{4,12},{8,16},{12,20},{16,24},{20,28},{24,0},{28,4},{1,9},{5... | collective-permute-start | bytes 786440 | tf_op jit(solution)/shard_map/ppermute | solution.py:164
  35.3 0.9 %copy-start = (bf16[8,64,768]{2,1,0:T(8,128)(2,1)}, bf16[8,64,768]{2,1,0:T(8,128)(2,1)S(1)}, u32[]{:S(2)}) copy-start(bf16[8,64,768]{2,1,0:T(8,128)(2,1)S(1)} %all-to-all-done) | copy-start | bytes 2359300
  36.2 1.1 %copy-start.1 = (bf16[8,64,768]{2,1,0:T(8,128)(2,1)S(1)}, bf16[8,64,768]{2,1,0:T(8,128)(2,1)}, u32[]{:S(2)}) copy-start(bf16[8,64,768]{2,1,0:T(8,128)(2,1)} %copy-done) | copy-start | bytes 2359300
  37.4 0.9 %copy-start.10 = (bf16[8,64,256]{2,1,0:T(8,128)(2,1)S(1)}, bf16[8,64,256]{2,1,0:T(8,128)(2,1)}, u32[]{:S(2)}) copy-start(bf16[8,64,256]{2,1,0:T(8,128)(2,1)} %copy-done.9) | copy-start | bytes 786436
  38.3 0.9 %copy-start.15 = (bf16[512,256]{1,0:T(8,128)(2,1)S(1)}, bf16[512,256]{1,0:T(8,128)(2,1)}, u32[]{:S(2)}) copy-start(bf16[512,256]{1,0:T(8,128)(2,1)} %copy-done.14) | copy-start | bytes 786436
  39.3 0.9 %copy-start.17 = (bf16[512,256]{1,0:T(8,128)(2,1)S(1)}, bf16[512,256]{1,0:T(8,128)(2,1)}, u32[]{:S(2)}) copy-start(bf16[512,256]{1,0:T(8,128)(2,1)} %copy-done.16) | copy-start | bytes 786436
  40.2 0.9 %copy-start.19 = (bf16[512,256]{1,0:T(8,128)(2,1)S(1)}, bf16[512,256]{1,0:T(8,128)(2,1)}, u32[]{:S(2)}) copy-start(bf16[512,256]{1,0:T(8,128)(2,1)} %copy-done.18) | copy-start | bytes 786436
  41.2 0.9 %copy-start.21 = (bf16[512,256]{1,0:T(8,128)(2,1)S(1)}, bf16[512,256]{1,0:T(8,128)(2,1)}, u32[]{:S(2)}) copy-start(bf16[512,256]{1,0:T(8,128)(2,1)} %copy-done.20) | copy-start | bytes 786436
  54.1 1.8 %collective-permute-start.6 = (bf16[512,256]{1,0:T(8,128)(2,1)S(1)}, bf16[512,256]{1,0:T(8,128)(2,1)S(1)}, u32[]{:S(2)}, u32[]{:S(2)}) collective-permute-start(bf16[512,256]{1,0:T(8,128)(2,1)S(1)} %collective-permute-done.5.refs_2_), channel_id=1, source_target_pairs={{0,1},{1,0},{2,3},{3,2},{4,5},{5,4},{6,7},{7,6},{8,9},{9,8},{10,11... | collective-permute-start | bytes 786440 | tf_op jit(solution)/shard_map/ppermute | solution.py:167
  55.9 2.6 %copy-start.5 = (bf16[512,256]{1,0:T(8,128)(2,1)}, bf16[512,256]{1,0:T(8,128)(2,1)S(1)}, u32[]{:S(2)}) copy-start(bf16[512,256]{1,0:T(8,128)(2,1)S(1)} %collective-permute-done.6.refs_3_) | copy-start | bytes 786436
  58.6 1.2 %copy-start.3 = (f32[2,4,384,128]{3,2,1,0:T(8,128)}, f32[2,4,384,128]{3,2,1,0:T(8,128)S(1)}, u32[]{:S(2)}) copy-start(f32[2,4,384,128]{3,2,1,0:T(8,128)S(1)} %get-tuple-element.33.refs_1_) | copy-start | bytes 4718596
  59.8 0.7 copy-start.8
  60.5 11.2 %all-to-all-start.2 = ((bf16[8,32,768]{2,1,0:T(8,128)(2,1)}), bf16[8,32,768]{2,1,0:T(8,128)(2,1)}, u32[]{:S(2)}, u32[]{:S(2)}) async-start(bf16[8,32,768]{2,1,0:T(8,128)(2,1)} %bitcast.22), calls=%async_computation.2 | async-start | bytes 786432 | tf_op jit(solution)/shard_map/all_to_all | solution.py:156
  64.9 1.1 %copy-start.2 = (bf16[8,64,768]{2,1,0:T(8,128)(2,1)S(1)}, bf16[8,64,768]{2,1,0:T(8,128)(2,1)}, u32[]{:S(2)}) copy-start(bf16[8,64,768]{2,1,0:T(8,128)(2,1)} %copy-done) | copy-start | bytes 2359300
  66.0 1.4 %copy-start.4 = (f32[2,4,384,128]{3,2,1,0:T(8,128)S(1)}, f32[2,4,384,128]{3,2,1,0:T(8,128)}, u32[]{:S(2)}) copy-start(f32[2,4,384,128]{3,2,1,0:T(8,128)} %copy-done.3) | copy-start | bytes 4718596
  67.4 0.9 %copy-start.6 = (bf16[512,256]{1,0:T(8,128)(2,1)S(1)}, bf16[512,256]{1,0:T(8,128)(2,1)}, u32[]{:S(2)}) copy-start(bf16[512,256]{1,0:T(8,128)(2,1)} %copy-done.5) | copy-start | bytes 786436
  71.0 0.7 copy-start.7
  71.7 10.8 %all-to-all-start.3 = ((bf16[8,32,768]{2,1,0:T(8,128)(2,1)}), bf16[8,32,768]{2,1,0:T(8,128)(2,1)S(1)}, u32[]{:S(2)}, u32[]{:S(2)}) async-start(bf16[8,32,768]{2,1,0:T(8,128)(2,1)} %bitcast.21), calls=%async_computation.3 | async-start | bytes 786432 | tf_op jit(solution)/shard_map/all_to_all | solution.py:156
where the time goes:
time: 84.1 us; the launch traced here: 84.4 us
  starting transfers between devices  26.4 us (31%)
  local copies, waits for them, and re-layouts  23.3 us (28%)
  Pallas kernels  17.2 us (20%)
  waiting for transfers between devices  15.9 us (19%)
  other arithmetic  1.37 us (2%)
    pallas_call x3, Pallas kernels, attend(): pl.pallas_call(functools.partial(attend_kernel, backs, blocks, state is N...  17.2 us
    all_to_all x4, starting transfers between devices, exchange(): lax.all_to_all(a, ('span', 'ctx'), 0, 0, axis_index_groups=planes, tiled=...  17.2 us
    unnamed x48, local copies, waits for them, and re-layouts  16.8 us
    all_to_all x4, waiting for transfers between devices, exchange(): lax.all_to_all(a, ('span', 'ctx'), 0, 0, axis_index_groups=planes, tiled=...  7.66 us
    ppermute x3, waiting for transfers between devices, up(): lax.ppermute(a, 'span', [(s, (s + 2 * steps) % spans) for s in range(span...  7.12 us
    ppermute x3, starting transfers between devices, up(): lax.ppermute(a, 'span', [(s, (s + 2 * steps) % spans) for s in range(span...  5.06 us
    ppermute x4, starting transfers between devices, near(): return lax.ppermute(a, 'ctx', other_core)  4.18 us
    reshape x3, local copies, waits for them, and re-layouts, by_head(): a = jnp.transpose(a.reshape(2, rows // 2, KVH, width), (2, 0, 1, 3))  3.88 us
  transfers between devices with their start and end apart: 11, of which 5 were waited for; matrix products, arithmetic and copies ran while one was open for 5% of the time, Pallas kernels for 17%

commit v1 on v0

v1 whole, which is shorter than its diff:
```python
import functools
import math

import jax
import jax.numpy as jnp
from jax import lax
from jax.experimental import pallas as pl
from jax.experimental.pallas import tpu as pltpu
from jax.sharding import PartitionSpec as P

HQ = 24
KVH = 4
HD = 128
GROUP = HQ // KVH
WIDE = GROUP * HD
PEERS = 8
LOW = -1e30
SCALE = math.log2(math.e) / math.sqrt(HD)
SMEM = pl.BlockSpec(memory_space=pltpu.SMEM)
VMEM = pl.BlockSpec(memory_space=pltpu.VMEM)
ANY = pl.BlockSpec(memory_space=pl.ANY)
SMALL = pltpu.CompilerParams(vmem_limit_bytes=6 << 20)
LARGE = pltpu.CompilerParams(vmem_limit_bytes=16 << 20)


def place():
    span, tok = lax.axis_index("span"), lax.axis_index("ctx")
    return span & -2, 4 * (span & 1) + tok


def begin_kernel(planes, levels_ref, temps_ref, list_ref, counts_ref, keys_ref, values_ref, *refs):
    kv_ref, table_ref, factor_ref, source, target, sems = refs
    loads = [
        pltpu.make_async_copy(ref, source.at[i], sems.at[i]) for i, ref in enumerate((keys_ref, values_ref))
    ]
    for load in loads:
        load.start()
    base, number = place()
    head = number >> 1
    for side in range(2):
        level = levels_ref[base + side]
        for i in range(GROUP):
            factor_ref[side * GROUP + i] = temps_ref[level, head * GROUP + i] * SCALE

        @pl.loop(0, 2 * planes)
        def _(slab):
            ident = base + (slab & 1) - 2 * (slab >> 1)
            found = base + side == ident
            for j in range(list_ref.shape[1]):
                found = found | (list_ref[base + side, j] == ident)
            count = jnp.where(found & (ident >= 0), counts_ref[jnp.maximum(ident, 0)], 0)
            table_ref[2 * slab + side] = count

    for load in loads:
        load.wait()
    part = source.shape[1] // 2
    for peer in range(PEERS):
        rows = slice((peer & 1) * part, (peer & 1) * part + part)
        lanes = slice((peer >> 1) * HD, (peer >> 1) * HD + HD)
        to = slice(peer * part, (peer + 1) * part)
        target[to, :HD] = source[0, rows, lanes]
        target[to, HD:] = source[1, rows, lanes]
    store = pltpu.make_async_copy(target, kv_ref, sems.at[0])
    store.start()
    store.wait()


def begin(planes, levels, temps, ctx_list, counts, keys, values):
    rows = keys.shape[0]
    shape = (PEERS * rows // 2, 2 * HD)
    return pl.pallas_call(
        functools.partial(begin_kernel, planes),
        out_shape=[
            jax.ShapeDtypeStruct(shape, jnp.bfloat16),
            jax.ShapeDtypeStruct((4 * planes,), jnp.int32),
            jax.ShapeDtypeStruct((2 * GROUP,), jnp.float32),
        ],
        in_specs=[SMEM] * 4 + [ANY] * 2,
        out_specs=[ANY, SMEM, SMEM],
        scratch_shapes=[
            pltpu.VMEM((2, *keys.shape), jnp.bfloat16),
            pltpu.VMEM(shape, jnp.bfloat16),
            pltpu.SemaphoreType.DMA((2,)),
        ],
        compiler_params=SMALL,
    )(levels, temps, ctx_list, counts, keys, values)


def cut_kernel(q_ref, *pieces):
    number = place()[1]
    part = q_ref.shape[0] // 2
    for j, piece in enumerate(pieces):
        peer = number ^ j
        rows = pl.ds(pl.multiple_of((peer & 1) * part, part), part)
        lanes = pl.ds(pl.multiple_of((peer >> 1) * WIDE, HD), WIDE)
        piece[...] = q_ref[rows, lanes]


def cut(q):
    return pl.pallas_call(
        cut_kernel,
        out_shape=[jax.ShapeDtypeStruct((q.shape[0] // 2, WIDE), jnp.bfloat16)] * PEERS,
        in_specs=[VMEM],
        out_specs=[VMEM] * PEERS,
        compiler_params=SMALL,
    )(q)


def join_kernel(*refs):
    pieces, out_ref, sems = refs[:PEERS], refs[PEERS], refs[PEERS + 1]
    number = place()[1]
    part = out_ref.shape[0] // 2
    copies = []
    for j, piece in enumerate(pieces):
        peer = number ^ j
        rows = pl.ds(pl.multiple_of((peer & 1) * part, part), part)
        lanes = pl.ds(pl.multiple_of((peer >> 1) * WIDE, HD), WIDE)
        copies.append(pltpu.make_async_copy(piece, out_ref.at[rows, lanes], sems.at[j]))
        copies[-1].start()
    for copy in copies:
        copy.wait()


def join(pieces):
    return pl.pallas_call(
        join_kernel,
        out_shape=jax.ShapeDtypeStruct((2 * pieces[0].shape[0], HQ * HD), jnp.bfloat16),
        in_specs=[VMEM] * PEERS,
        out_specs=ANY,
        scratch_shapes=[pltpu.SemaphoreType.DMA((PEERS,))],
        compiler_params=SMALL,
    )(*pieces)


def attend_kernel(backs, first, final, table_ref, factor_ref, *refs):
    refs = list(refs)
    if first:
        q_pieces = [refs.pop(0) for _ in range(PEERS)]
    else:
        q_ref = refs.pop(0)
        del refs[:2]
    slabs = [(refs.pop(0), refs.pop(0)) for _ in backs]
    out_refs = [refs.pop(0) for _ in range(PEERS)] if final else None
    sums_ref, top_ref = refs.pop(0), refs.pop(0)
    number = place()[1]
    core = number & 1
    if first:
        q_ref = refs.pop(0)
        for j, piece in enumerate(q_pieces):
            q_ref[number ^ j] = piece[...]
        sums_ref[...] = jnp.zeros_like(sums_ref)
        top_ref[...] = jnp.full_like(top_ref, LOW)
    key_ref, value_ref = refs[:2]
    piece = q_ref.shape[1]
    half = slabs[0][0].shape[0] // 2
    group = GROUP // 2
    chains = [(block, g) for block in range(2) for g in range(2)]

    index = lax.broadcasted_iota(jnp.int32, (half, HD), 0)
    for slab, back in zip(slabs, backs):
        for x in range(2):
            count = jnp.maximum(table_ref[4 * back + 2 * x], table_ref[4 * back + 2 * x + 1])
            spare = slab[0][x * half : x * half + 16, :HD].astype(jnp.float32)[0:1]
            for side, ref in enumerate(slab):
                token = (index // piece) * (2 * piece) + (core ^ side) * piece + index % piece
                keep = token < count
                at = slice(x * half, (x + 1) * half)
                to = slice(side * half, (side + 1) * half)
                keys = jnp.where(keep, ref[at, :HD].astype(jnp.float32), spare)
                values = jnp.where(keep, ref[at, HD:].astype(jnp.float32), 0.0)
                key_ref[x, :, to] = jnp.transpose(keys).astype(jnp.bfloat16)
                value_ref[x, to, :HD] = values.astype(jnp.bfloat16)
                value_ref[x, to, HD:] = jnp.where(keep, 1.0, 0.0).astype(jnp.bfloat16)

        @pl.loop(0, 4)
        def _(turn):
            x = turn >> 1
            side = turn & 1

            @pl.when(table_ref[4 * back + turn] > 0)
            def _():
                keys = key_ref[x]
                values = value_ref[x]

                def scores(block, g):
                    rows = []
                    for i in range(group):
                        lanes = slice((g * group + i) * HD, (g * group + i + 1) * HD)
                        for t in range(2):
                            rows.append(q_ref[4 * side + 2 * block + t, :, lanes])
                    return jnp.dot(jnp.concatenate(rows, axis=0), keys, preferred_element_type=jnp.float32)

                ready = scores(*chains[0])
                for n, (block, g) in enumerate(chains):
                    s = ready
                    if n + 1 < len(chains):
                        ready = scores(*chains[n + 1])
                    step = s.shape[0] // group
                    s = jnp.concatenate(
                        [
                            s[i * step : (i + 1) * step] * factor_ref[side * GROUP + g * group + i]
                            for i in range(group)
                        ],
                        axis=0,
                    )
                    chain = 2 * block + g
                    old_top = top_ref[side, chain]
                    top = jnp.maximum(old_top, jnp.max(s, axis=1, keepdims=True))
                    weight = jnp.concatenate(
                        [jnp.exp2(s[:, at : at + HD] - top).astype(jnp.bfloat16) for at in range(0, s.shape[1], HD)],
                        axis=1,
                    )
                    sums = jnp.dot(weight, values, preferred_element_type=jnp.float32)
                    shrink = jnp.exp2(old_top - top)
                    sums_ref[side, chain] = sums + sums_ref[side, chain] * jnp.concatenate([shrink, shrink], axis=1)
                    top_ref[side, chain] = top

    if final:
        done_ref = refs[2]
        for side in range(2):
            for block, g in chains:
                sums = sums_ref[side, 2 * block + g]
                result = (sums[:, :HD] / sums[:, HD:]).astype(jnp.bfloat16)
                for i in range(group):
                    lanes = slice((g * group + i) * HD, (g * group + i + 1) * HD)
                    for t in range(2):
                        at = (2 * i + t) * piece
                        done_ref[4 * side + 2 * block + t, :, lanes] = result[at : at + piece]
        for j, out_ref in enumerate(out_refs):
            out_ref[...] = done_ref[number ^ j]


def attend(tables, q, state, slabs, backs, final):
    first = state is None
    piece = q[0].shape[-2]
    tall = GROUP * piece
    tokens = slabs[0][0].shape[0]
    q_shape = (PEERS, piece, WIDE)
    out_shape = [
        jax.ShapeDtypeStruct((2, 4, tall, 2 * HD), jnp.float32),
        jax.ShapeDtypeStruct((2, 4, tall, HD), jnp.float32),
    ]
    scratch = [pltpu.VMEM((2, HD, tokens), jnp.bfloat16), pltpu.VMEM((2, tokens, 2 * HD), jnp.bfloat16)]
    if final:
        out_shape = [jax.ShapeDtypeStruct(q_shape[1:], jnp.bfloat16)] * PEERS + out_shape
        scratch.append(pltpu.VMEM(q_shape, jnp.bfloat16))
    if first:
        out_shape.append(jax.ShapeDtypeStruct(q_shape, jnp.bfloat16))
    work = len(backs) * PEERS * tall * tokens
    inputs = [*q, *(state or ()), *[a for slab in slabs for a in slab]]
    aliases = {} if first else {3: PEERS * final, 4: PEERS * final + 1}
    return pl.pallas_call(
        functools.partial(attend_kernel, backs, first, final),
        out_shape=out_shape,
        in_specs=[SMEM] * 2 + [VMEM] * len(inputs),
        out_specs=[VMEM] * len(out_shape),
        scratch_shapes=scratch,
        input_output_aliases=aliases,
        compiler_params=LARGE,
        cost_estimate=pl.CostEstimate(flops=2 * work * HD, bytes_accessed=4 * PEERS * piece * WIDE, transcendentals=work // 2),
    )(*tables, *inputs)


def per_device(spans, ctx, queries, keys, values, temps, levels, ctx_list, counts):
    planes = [list(range(p * ctx, (p + 2) * ctx)) for p in range(0, spans, 2)]
    other_core = [(t, t ^ 1) for t in range(ctx)]
    last = spans // 2 - 1

    def swap(pieces):
        moved = [pieces[0]]
        for j in range(1, PEERS):
            moved.append(lax.ppermute(pieces[j], ("span", "ctx"), [(f, f ^ j) for f in range(spans * ctx)]))
        return moved

    def up(a, steps):
        return lax.ppermute(a, "span", [(s, (s + 2 * steps) % spans) for s in range(spans)])

    def near(a):
        return lax.ppermute(a, "ctx", other_core)

    kv, *tables = begin(spans // 2, levels, temps, ctx_list, counts, keys, values)
    own = lax.all_to_all(kv, ("span", "ctx"), 0, 0, axis_index_groups=planes, tiled=True)
    slabs = {0: own, 1: up(own, 1), last: up(own, last)}
    q = swap(cut(queries))
    others = {back: near(slab) for back, slab in slabs.items()}
    slabs, others = lax.optimization_barrier((slabs, others))
    stage = sorted(slabs)
    state = None
    for back in range(2, last):
        *state, q_all = [*attend(tables, q, state, [(slabs[b], others[b]) for b in stage], stage, False), *q][:3]
        q = [q_all]
        slabs[back] = up(slabs[back - 1], 1)
        slabs[back], state = lax.optimization_barrier((slabs[back], state))
        others[back] = near(slabs[back])
        stage = [back]
    out = attend(tables, q, state, [(slabs[b], others[b]) for b in stage], stage, True)
    return join(swap(out[:PEERS]))


def solution(mesh):
    return jax.shard_map(
        functools.partial(per_device, mesh.shape["span"], mesh.shape["ctx"]),
        mesh=mesh,
        in_specs=(
            P(("span", "ctx"), None),
            P(("span", "ctx"), None),
            P(("span", "ctx"), None),
            P(),
            P(),
            P(),
            P(),
        ),
        out_specs=P(("span", "ctx"), None),
        check_vma=False,
    )
```

time: 84.1 us -> 76.9 us (0.914); the launches traced: 84.4 us -> 75.9 us
  local copies, waits for them, and re-layouts: 23.3 us -> 5.69 us
  blocking collectives: 0 us -> 9.49 us
  waiting for transfers between devices: 15.9 us -> 19.4 us
  Pallas kernels: 17.2 us -> 15.8 us
  other arithmetic: 1.37 us -> 0 us
  starting transfers between devices: 26.4 us -> 25.5 us
    all_to_all x4 -> x0, starting transfers between devices: 17.2 us -> none  [exchange(): lax.all_to_all(a, ('span', 'ctx'), 0, 0, axis_index_groups=planes, tiled=...]
    ppermute x0 -> x14, starting transfers between devices: none -> 14.1 us  [swap(): lax.ppermute(pieces[j], ('span', 'ctx'), [(f, f ^ j) for f in range(spans...]
    ppermute x0 -> x14, waiting for transfers between devices: none -> 12.9 us  [swap(): lax.ppermute(pieces[j], ('span', 'ctx'), [(f, f ^ j) for f in range(spans...]
    unnamed x48 -> x13, local copies, waits for them, and re-layouts: 16.8 us -> 5.69 us
    all_to_all x0 -> x1, blocking collectives: none -> 9.49 us  [per_device(): lax.all_to_all(kv, ('span', 'ctx'), 0, 0, axis_index_groups=planes, tiled...]
    all_to_all x4 -> x0, waiting for transfers between devices: 7.66 us -> none  [exchange(): lax.all_to_all(a, ('span', 'ctx'), 0, 0, axis_index_groups=planes, tiled=...]
    reshape x5 -> x0, local copies, waits for them, and re-layouts: 5.49 us -> none  [the longest x3 3.88 us: by_head(): a = jnp.transpose(a.reshape(2, rows // 2, KVH, width), (2, 0, 1, 3))]
    ppermute x4, starting transfers between devices: 4.18 us -> 6.39 us  [near(): return lax.ppermute(a, 'ctx', other_core)]
  transfers between devices with their start and end apart: 11 -> 21, of which waited for: 5 -> 10; matrix products, arithmetic and copies ran while one was open for 5% -> 0% of each run, Pallas kernels for 17% -> 14%
where the time goes in v1:
time: 76.9 us; the launch traced here: 75.9 us
  starting transfers between devices  25.5 us (33%)
  waiting for transfers between devices  19.4 us (25%)
  Pallas kernels  15.8 us (21%)
  blocking collectives  9.49 us (12%)
  local copies, waits for them, and re-layouts  5.69 us (7%)
    ppermute x14, starting transfers between devices, swap(): lax.ppermute(pieces[j], ('span', 'ctx'), [(f, f ^ j) for f in range(spans...  14.1 us
    ppermute x14, waiting for transfers between devices, swap(): lax.ppermute(pieces[j], ('span', 'ctx'), [(f, f ^ j) for f in range(spans...  12.9 us
    pallas_call x2, Pallas kernels, attend(): pl.pallas_call(functools.partial(attend_kernel, backs, first, final), out...  12.8 us
    all_to_all x1, blocking collectives, per_device(): lax.all_to_all(kv, ('span', 'ctx'), 0, 0, axis_index_groups=planes, tiled...  9.49 us
    ppermute x4, starting transfers between devices, near(): return lax.ppermute(a, 'ctx', other_core)  6.39 us
    unnamed x13, local copies, waits for them, and re-layouts  5.69 us
    ppermute x3, waiting for transfers between devices, up(): lax.ppermute(a, 'span', [(s, (s + 2 * steps) % spans) for s in range(span...  5.15 us
    ppermute x3, starting transfers between devices, up(): lax.ppermute(a, 'span', [(s, (s + 2 * steps) % spans) for s in range(span...  5.06 us
  transfers between devices with their start and end apart: 21, of which 10 were waited for; matrix products, arithmetic and copies ran while one was open for 0% of the time, Pallas kernels for 14%

profile of v1, /device:TPU:25, one launch (start us, length us, event | category | flops | bytes accessed | tf_op | source)
XLA Modules:
  0.0 75.9 jit_solution(8793927296158293822)
XLA Ops:
  0.0 0.8 copy.10.list_ref
  0.8 0.0 copy-start.1
  0.8 0.9 %copy-done.1 = bf16[128,512]{1,0:T(8,128)(2,1)S(1)} copy-done((bf16[128,512]{1,0:T(8,128)(2,1)S(1)}, bf16[128,512]{1,0:T(8,128)(2,1)}, u32[]{:S(2)}) %copy-start.1) | copy-done | bytes 131096
  1.7 0.0 copy-start.2
  1.7 0.9 %copy-done.2 = bf16[128,512]{1,0:T(8,128)(2,1)S(1)} copy-done((bf16[128,512]{1,0:T(8,128)(2,1)S(1)}, bf16[128,512]{1,0:T(8,128)(2,1)}, u32[]{:S(2)}) %copy-start.2) | copy-done | bytes 131096
  2.6 0.0 copy-start.3
  2.6 0.7 copy-done.3
  3.3 0.0 copy-start.4
  3.3 0.7 copy-done.4
  3.9 0.0 copy-start.5
  3.9 0.7 copy-done.5
  4.6 2.0 %shard_map.73 = (bf16[512,256]{1,0:T(8,128)(2,1)S(1)}, s32[16]{0:T(128)S(1)}, f32[12]{0:T(128)S(1)}) custom-call(s32[8]{0:T(128)S(1)} %copy-done.4, f32[8,24]{1,0:T(8,128)S(1)} %copy-done.3, s32[8,4]{1,0:T(8,128)S(1)} %copy.10.list_ref, s32[8]{0:T(128)S(1)} %copy-done.5, bf16[128,512]{1,0:T(8,128)(2,1)S(1)} %copy-done.1, bf16[128,512]{1,0:T(8,128)(2,1)S(1)} %copy-done.2), custom_call_target="tpu_custom_call" | custom-call | tf_op jit(solution)/shard_map/pallas_call | solution.py:71
  6.5 9.5 %all_to_all.12 = bf16[8,64,256]{2,1,0:T(8,128)(2,1)S(1)} all-to-all(bf16[8,64,256]{2,1,0:T(8,128)(2,1)S(1)} %bitcast.6), channel_id=1, replica_groups={{0,1,2,3,4,5,6,7},{8,9,10,11,12,13,14,15},{16,17,18,19,20,21,22,23},{24..., dimensions={0} | all-to-all | bytes 524288 | tf_op jit(solution)/shard_map/all_to_all | solution.py:282
  16.0 0.2 collective-permute-start.8
  16.2 3.1 %collective-permute-start.7 = (bf16[512,256]{1,0:T(8,128)(2,1)S(1)}, bf16[512,256]{1,0:T(8,128)(2,1)S(1)}, u32[]{:S(2)}, u32[]{:S(2)}) collective-permute-start(bf16[512,256]{1,0:T(8,128)(2,1)S(1)} %bitcast.3), channel_id=1, source_target_pairs={{0,8},{4,12},{8,16},{12,20},{16,24},{20,28},{24,0},{28,4},{1,9},{5... | collective-permute-start | bytes 786440 | tf_op jit(solution)/shard_map/ppermute | solution.py:276
  19.3 1.3 %collective-permute-start.9 = (bf16[512,256]{1,0:T(8,128)(2,1)S(1)}, bf16[512,256]{1,0:T(8,128)(2,1)S(1)}, u32[]{:S(2)}, u32[]{:S(2)}) collective-permute-start(bf16[512,256]{1,0:T(8,128)(2,1)S(1)} %bitcast.4), channel_id=1, source_target_pairs={{0,1},{1,0},{2,3},{3,2},{4,5},{5,4},{6,7},{7,6},{8,9},{9,8},{10,11... | collective-permute-start | bytes 786440 | tf_op jit(solution)/shard_map/ppermute | solution.py:279
  20.6 4.4 %collective-permute-done.8.refs_12_ = bf16[512,256]{1,0:T(8,128)(2,1)S(1)} collective-permute-done((bf16[512,256]{1,0:T(8,128)(2,1)S(1)}, bf16[512,256]{1,0:T(8,128)(2,1)S(1)}, u32[]{:S(2)}, u32[]{:S(2)}) %collective-permute-start.8) | collective-permute-done | bytes 262176 | tf_op jit(solution)/shard_map/ppermute | solution.py:276
  25.0 2.8 %collective-permute-start.11 = (bf16[512,256]{1,0:T(8,128)(2,1)S(1)}, bf16[512,256]{1,0:T(8,128)(2,1)S(1)}, u32[]{:S(2)}, u32[]{:S(2)}) collective-permute-start(bf16[512,256]{1,0:T(8,128)(2,1)S(1)} %collective-permute-done.8.refs_12_), channel_id=1, source_target_pairs={{0,1},{1,0},{2,3},{3,2},{4,5},{5,4},{6,7},{7,6},{8,9},{9,8},{10,11... | collective-permute-start | bytes 786440 | tf_op jit(solution)/shard_map/ppermute | solution.py:279
  27.8 0.8 %collective-permute-done.7.refs_10_ = bf16[512,256]{1,0:T(8,128)(2,1)S(1)} collective-permute-done((bf16[512,256]{1,0:T(8,128)(2,1)S(1)}, bf16[512,256]{1,0:T(8,128)(2,1)S(1)}, u32[]{:S(2)}, u32[]{:S(2)}) %collective-permute-start.7) | collective-permute-done | bytes 262176 | tf_op jit(solution)/shard_map/ppermute | solution.py:276
  28.6 2.0 %collective-permute-start.10 = (bf16[512,256]{1,0:T(8,128)(2,1)S(1)}, bf16[512,256]{1,0:T(8,128)(2,1)S(1)}, u32[]{:S(2)}, u32[]{:S(2)}) collective-permute-start(bf16[512,256]{1,0:T(8,128)(2,1)S(1)} %collective-permute-done.7.refs_10_), channel_id=1, source_target_pairs={{0,1},{1,0},{2,3},{3,2},{4,5},{5,4},{6,7},{7,6},{8,9},{9,8},{10,11... | collective-permute-start | bytes 786440 | tf_op jit(solution)/shard_map/ppermute | solution.py:279
  30.5 0.0 copy-start
  30.5 1.1 %copy-done = bf16[128,3072]{1,0:T(8,128)(2,1)S(1)} copy-done((bf16[128,3072]{1,0:T(8,128)(2,1)S(1)}, bf16[128,3072]{1,0:T(8,128)(2,1)}, u32[]{:S(2)}) %copy-start) | copy-done | bytes 786456
  31.7 0.1 shard_map.74
  31.7 0.1 collective-permute-start
  31.8 1.0 %collective-permute-start.1 = (bf16[64,768]{1,0:T(8,128)(2,1)S(1)}, bf16[64,768]{1,0:T(8,128)(2,1)S(1)}, u32[]{:S(2)}, u32[]{:S(2)}) collective-permute-start(bf16[64,768]{1,0:T(8,128)(2,1)S(1)} %get-tuple-element.40), channel_id=1, source_target_pairs={{0,2},{1,3},{2,0},{3,1},{4,6},{5,7},{6,4},{7,5},{8,10},{9,11},{10,... | collective-permute-start | bytes 294920 | tf_op jit(solution)/shard_map/ppermute | solution.py:272
  32.8 0.0 collective-permute-done.9.refs_9_
  32.8 1.1 %collective-permute-start.2 = (bf16[64,768]{1,0:T(8,128)(2,1)S(1)}, bf16[64,768]{1,0:T(8,128)(2,1)S(1)}, u32[]{:S(2)}, u32[]{:S(2)}) collective-permute-start(bf16[64,768]{1,0:T(8,128)(2,1)S(1)} %get-tuple-element.41), channel_id=1, source_target_pairs={{0,3},{1,2},{2,1},{3,0},{4,7},{5,6},{6,5},{7,4},{8,11},{9,10},{10,... | collective-permute-start | bytes 294920 | tf_op jit(solution)/shard_map/ppermute | solution.py:272
  33.9 0.0 collective-permute-done.11.refs_13_
  33.9 0.0 collective-permute-done.10.refs_11_
  33.9 1.8 %collective-permute-start.12 = (bf16[512,256]{1,0:T(8,128)(2,1)S(1)}, bf16[512,256]{1,0:T(8,128)(2,1)S(1)}, u32[]{:S(2)}, u32[]{:S(2)}) collective-permute-start(bf16[512,256]{1,0:T(8,128)(2,1)S(1)} %collective-permute-done.7.refs_10_), channel_id=1, source_target_pairs={{0,8},{4,12},{8,16},{12,20},{16,24},{20,28},{24,0},{28,4},{1,9},{5... | collective-permute-start | bytes 786440 | tf_op jit(solution)/shard_map/ppermute | solution.py:276
  35.7 1.2 %collective-permute-start.3 = (bf16[64,768]{1,0:T(8,128)(2,1)S(1)}, bf16[64,768]{1,0:T(8,128)(2,1)S(1)}, u32[]{:S(2)}, u32[]{:S(2)}) collective-permute-start(bf16[64,768]{1,0:T(8,128)(2,1)S(1)} %get-tuple-element.42), channel_id=1, source_target_pairs={{0,4},{1,5},{2,6},{3,7},{4,0},{5,1},{6,2},{7,3},{8,12},{9,13},{10,... | collective-permute-start | bytes 294920 | tf_op jit(solution)/shard_map/ppermute | solution.py:272
  36.9 0.0 collective-permute-done.refs_1_
  36.9 0.5 collective-permute-start.4
  37.5 0.0 collective-permute-done.1.refs_2_
  37.5 1.3 %collective-permute-start.5 = (bf16[64,768]{1,0:T(8,128)(2,1)S(1)}, bf16[64,768]{1,0:T(8,128)(2,1)S(1)}, u32[]{:S(2)}, u32[]{:S(2)}) collective-permute-start(bf16[64,768]{1,0:T(8,128)(2,1)S(1)} %get-tuple-element.44), channel_id=1, source_target_pairs={{0,6},{1,7},{2,4},{3,5},{4,2},{5,3},{6,0},{7,1},{8,14},{9,15},{10,... | collective-permute-start | bytes 294920 | tf_op jit(solution)/shard_map/ppermute | solution.py:272
  38.7 0.1 collective-permute-done.2.refs_3_
  38.8 1.4 %collective-permute-start.6 = (bf16[64,768]{1,0:T(8,128)(2,1)S(1)}, bf16[64,768]{1,0:T(8,128)(2,1)S(1)}, u32[]{:S(2)}, u32[]{:S(2)}) collective-permute-start(bf16[64,768]{1,0:T(8,128)(2,1)S(1)} %get-tuple-element.45), channel_id=1, source_target_pairs={{0,7},{1,6},{2,5},{3,4},{4,3},{5,2},{6,1},{7,0},{8,15},{9,14},{10,... | collective-permute-start | bytes 294920 | tf_op jit(solution)/shard_map/ppermute | solution.py:272
  40.2 0.0 collective-permute-done.3.refs_4_
  40.2 2.6 %collective-permute-done.4.refs_5_ = bf16[64,768]{1,0:T(8,128)(2,1)S(1)} collective-permute-done((bf16[64,768]{1,0:T(8,128)(2,1)S(1)}, bf16[64,768]{1,0:T(8,128)(2,1)S(1)}, u32[]{:S(2)}, u32[]{:S(2)}) %collective-permute-start.4) | collective-permute-done | bytes 98336 | tf_op jit(solution)/shard_map/ppermute | solution.py:272
  42.8 2.1 %collective-permute-done.5.refs_6_ = bf16[64,768]{1,0:T(8,128)(2,1)S(1)} collective-permute-done((bf16[64,768]{1,0:T(8,128)(2,1)S(1)}, bf16[64,768]{1,0:T(8,128)(2,1)S(1)}, u32[]{:S(2)}, u32[]{:S(2)}) %collective-permute-start.5) | collective-permute-done | bytes 98336 | tf_op jit(solution)/shard_map/ppermute | solution.py:272
  45.0 2.3 %collective-permute-done.6.refs_7_ = bf16[64,768]{1,0:T(8,128)(2,1)S(1)} collective-permute-done((bf16[64,768]{1,0:T(8,128)(2,1)S(1)}, bf16[64,768]{1,0:T(8,128)(2,1)S(1)}, u32[]{:S(2)}, u32[]{:S(2)}) %collective-permute-start.6) | collective-permute-done | bytes 98336 | tf_op jit(solution)/shard_map/ppermute | solution.py:272
  47.2 10.5 %shard_map.75 = (f32[2,4,384,256]{3,2,1,0:T(8,128)S(1)}, f32[2,4,384,128]{3,2,1,0:T(8,128)S(1)}, bf16[8,64,768]{2,1,0:T(8,128)(2,1)S(1)}) custom-call(s32[16]{0:T(128)S(1)} %get-tuple-element.36.table_ref, f32[12]{0:T(128)S(1)} %get-tuple-element.37.factor_ref, bf16[64,768]{1,0:T(8,128)(2,1)S(1)} %get-tuple-element.38.refs_0_, ...), custom_call_target="tpu_custom_call" | custom-call | flops 1207959552 | bytes 1572864 | tf_op jit(solution)/shard_map/pallas_call | solution.py:252
  57.7 0.0 collective-permute-done.12.refs_3_
  57.7 0.3 collective-permute-start.13
  58.0 1.3 %collective-permute-done.13.refs_4_ = bf16[512,256]{1,0:T(8,128)(2,1)S(1)} collective-permute-done((bf16[512,256]{1,0:T(8,128)(2,1)S(1)}, bf16[512,256]{1,0:T(8,128)(2,1)S(1)}, u32[]{:S(2)}, u32[]{:S(2)}) %collective-permute-start.13) | collective-permute-done | bytes 262176 | tf_op jit(solution)/shard_map/ppermute | solution.py:279
  59.3 2.4 %shard_map.76 = (bf16[64,768]{1,0:T(8,128)(2,1)S(1)}, bf16[64,768]{1,0:T(8,128)(2,1)S(1)}, bf16[64,768]{1,0:T(8,128)(2,1)S(1)}, bf16[64,768]{1,0:T(8,128)(2,1)S(...) custom-call(s32[16]{0:T(128)S(1)} %get-tuple-element.36.table_ref, ...), custom_call_target="tpu_custom_call", output_to_operand_aliasing={{8}: (3, {}), {9}: (4, {})} | custom-call | flops 402653184 | bytes 1572864 | tf_op jit(solution)/shard_map/pallas_call | solution.py:252
  61.7 0.3 collective-permute-start.14
  62.0 0.5 collective-permute-start.15
  62.5 1.4 %collective-permute-start.16 = (bf16[64,768]{1,0:T(8,128)(2,1)S(1)}, bf16[64,768]{1,0:T(8,128)(2,1)S(1)}, u32[]{:S(2)}, u32[]{:S(2)}) collective-permute-start(bf16[64,768]{1,0:T(8,128)(2,1)S(1)} %get-tuple-element.62), channel_id=1, source_target_pairs={{0,3},{1,2},{2,1},{3,0},{4,7},{5,6},{6,5},{7,4},{8,11},{9,10},{10,... | collective-permute-start | bytes 294920 | tf_op jit(solution)/shard_map/ppermute | solution.py:272
  63.9 0.6 collective-permute-start.17
  64.5 1.0 %collective-permute-start.18 = (bf16[64,768]{1,0:T(8,128)(2,1)S(1)}, bf16[64,768]{1,0:T(8,128)(2,1)S(1)}, u32[]{:S(2)}, u32[]{:S(2)}) collective-permute-start(bf16[64,768]{1,0:T(8,128)(2,1)S(1)} %get-tuple-element.64), channel_id=1, source_target_pairs={{0,5},{1,4},{2,7},{3,6},{4,1},{5,0},{6,3},{7,2},{8,13},{9,12},{10,... | collective-permute-start | bytes 294920 | tf_op jit(solution)/shard_map/ppermute | solution.py:272
  65.5 0.0 collective-permute-done.14.refs_1_
  65.5 1.4 %collective-permute-start.19 = (bf16[64,768]{1,0:T(8,128)(2,1)S(1)}, bf16[64,768]{1,0:T(8,128)(2,1)S(1)}, u32[]{:S(2)}, u32[]{:S(2)}) collective-permute-start(bf16[64,768]{1,0:T(8,128)(2,1)S(1)} %get-tuple-element.65), channel_id=1, source_target_pairs={{0,6},{1,7},{2,4},{3,5},{4,2},{5,3},{6,0},{7,1},{8,14},{9,15},{10,... | collective-permute-start | bytes 294920 | tf_op jit(solution)/shard_map/ppermute | solution.py:272
  66.9 0.0 collective-permute-done.15.refs_2_
  66.9 2.3 %collective-permute-start.20 = (bf16[64,768]{1,0:T(8,128)(2,1)S(1)}, bf16[64,768]{1,0:T(8,128)(2,1)S(1)}, u32[]{:S(2)}, u32[]{:S(2)}) collective-permute-start(bf16[64,768]{1,0:T(8,128)(2,1)S(1)} %get-tuple-element.66), channel_id=1, source_target_pairs={{0,7},{1,6},{2,5},{3,4},{4,3},{5,2},{6,1},{7,0},{8,15},{9,14},{10,... | collective-permute-start | bytes 294920 | tf_op jit(solution)/shard_map/ppermute | solution.py:272
  69.2 0.0 collective-permute-done.16.refs_3_
  69.2 0.0 collective-permute-done.17.refs_4_
  69.2 1.7 %collective-permute-done.18.refs_5_ = bf16[64,768]{1,0:T(8,128)(2,1)S(1)} collective-permute-done((bf16[64,768]{1,0:T(8,128)(2,1)S(1)}, bf16[64,768]{1,0:T(8,128)(2,1)S(1)}, u32[]{:S(2)}, u32[]{:S(2)}) %collective-permute-start.18) | collective-permute-done | bytes 98336 | tf_op jit(solution)/shard_map/ppermute | solution.py:272
  70.9 2.0 %collective-permute-done.19.refs_6_ = bf16[64,768]{1,0:T(8,128)(2,1)S(1)} collective-permute-done((bf16[64,768]{1,0:T(8,128)(2,1)S(1)}, bf16[64,768]{1,0:T(8,128)(2,1)S(1)}, u32[]{:S(2)}, u32[]{:S(2)}) %collective-permute-start.19) | collective-permute-done | bytes 98336 | tf_op jit(solution)/shard_map/ppermute | solution.py:272
  72.9 2.1 %collective-permute-done.20.refs_7_ = bf16[64,768]{1,0:T(8,128)(2,1)S(1)} collective-permute-done((bf16[64,768]{1,0:T(8,128)(2,1)S(1)}, bf16[64,768]{1,0:T(8,128)(2,1)S(1)}, u32[]{:S(2)}, u32[]{:S(2)}) %collective-permute-start.20) | collective-permute-done | bytes 98336 | tf_op jit(solution)/shard_map/ppermute | solution.py:272
  75.0 0.9 %shard_map.77 = bf16[128,3072]{1,0:T(8,128)(2,1)} custom-call(bf16[64,768]{1,0:T(8,128)(2,1)S(1)} %get-tuple-element.59.refs_0_, bf16[64,768]{1,0:T(8,128)(2,1)S(1)} %collective-permute-done.14.refs_1_, bf16[64,768]{1,0:T(8,128)(2,1)S(1)} %collective-permute-done.15.refs_2_, bf16[64,768]{1,0:T(8,128)(2,1)S(1)} %collective-permute-done.16.refs_3_, ...), custom_call_target="tpu_custom_call" | custom-call | tf_op jit(solution)/shard_map/pallas_call | solution.py:125
Async XLA Ops:
  0.8 0.9 %copy-start.1 = (bf16[128,512]{1,0:T(8,128)(2,1)S(1)}, bf16[128,512]{1,0:T(8,128)(2,1)}, u32[]{:S(2)}) copy-start(bf16[128,512]{1,0:T(8,128)(2,1)} %keys_ref.1) | copy-start | bytes 393220
  1.7 0.9 %copy-start.2 = (bf16[128,512]{1,0:T(8,128)(2,1)S(1)}, bf16[128,512]{1,0:T(8,128)(2,1)}, u32[]{:S(2)}) copy-start(bf16[128,512]{1,0:T(8,128)(2,1)} %values_ref.1) | copy-start | bytes 393220
  2.6 0.7 copy-start.3
  3.3 0.7 copy-start.4
  3.9 0.7 copy-start.5
  16.0 9.0 %collective-permute-start.8 = (bf16[512,256]{1,0:T(8,128)(2,1)S(1)}, bf16[512,256]{1,0:T(8,128)(2,1)S(1)}, u32[]{:S(2)}, u32[]{:S(2)}) collective-permute-start(bf16[512,256]{1,0:T(8,128)(2,1)S(1)} %bitcast.2), channel_id=1, source_target_pairs={{0,24},{4,28},{8,0},{12,4},{16,8},{20,12},{24,16},{28,20},{1,25},{... | collective-permute-start | bytes 786440 | tf_op jit(solution)/shard_map/ppermute | solution.py:276
  16.2 12.4 %collective-permute-start.7 = (bf16[512,256]{1,0:T(8,128)(2,1)S(1)}, bf16[512,256]{1,0:T(8,128)(2,1)S(1)}, u32[]{:S(2)}, u32[]{:S(2)}) collective-permute-start(bf16[512,256]{1,0:T(8,128)(2,1)S(1)} %bitcast.3), channel_id=1, source_target_pairs={{0,8},{4,12},{8,16},{12,20},{16,24},{20,28},{24,0},{28,4},{1,9},{5... | collective-permute-start | bytes 786440 | tf_op jit(solution)/shard_map/ppermute | solution.py:276
  19.3 13.5 %collective-permute-start.9 = (bf16[512,256]{1,0:T(8,128)(2,1)S(1)}, bf16[512,256]{1,0:T(8,128)(2,1)S(1)}, u32[]{:S(2)}, u32[]{:S(2)}) collective-permute-start(bf16[512,256]{1,0:T(8,128)(2,1)S(1)} %bitcast.4), channel_id=1, source_target_pairs={{0,1},{1,0},{2,3},{3,2},{4,5},{5,4},{6,7},{7,6},{8,9},{9,8},{10,11... | collective-permute-start | bytes 786440 | tf_op jit(solution)/shard_map/ppermute | solution.py:279
  25.0 8.9 %collective-permute-start.11 = (bf16[512,256]{1,0:T(8,128)(2,1)S(1)}, bf16[512,256]{1,0:T(8,128)(2,1)S(1)}, u32[]{:S(2)}, u32[]{:S(2)}) collective-permute-start(bf16[512,256]{1,0:T(8,128)(2,1)S(1)} %collective-permute-done.8.refs_12_), channel_id=1, source_target_pairs={{0,1},{1,0},{2,3},{3,2},{4,5},{5,4},{6,7},{7,6},{8,9},{9,8},{10,11... | collective-permute-start | bytes 786440 | tf_op jit(solution)/shard_map/ppermute | solution.py:279
  28.6 5.4 %collective-permute-start.10 = (bf16[512,256]{1,0:T(8,128)(2,1)S(1)}, bf16[512,256]{1,0:T(8,128)(2,1)S(1)}, u32[]{:S(2)}, u32[]{:S(2)}) collective-permute-start(bf16[512,256]{1,0:T(8,128)(2,1)S(1)} %collective-permute-done.7.refs_10_), channel_id=1, source_target_pairs={{0,1},{1,0},{2,3},{3,2},{4,5},{5,4},{6,7},{7,6},{8,9},{9,8},{10,11... | collective-permute-start | bytes 786440 | tf_op jit(solution)/shard_map/ppermute | solution.py:279
  30.5 1.1 %copy-start = (bf16[128,3072]{1,0:T(8,128)(2,1)S(1)}, bf16[128,3072]{1,0:T(8,128)(2,1)}, u32[]{:S(2)}) copy-start(bf16[128,3072]{1,0:T(8,128)(2,1)} %q_ref.1) | copy-start | bytes 2359300
  31.7 5.2 %collective-permute-start = (bf16[64,768]{1,0:T(8,128)(2,1)S(1)}, bf16[64,768]{1,0:T(8,128)(2,1)S(1)}, u32[]{:S(2)}, u32[]{:S(2)}) collective-permute-start(bf16[64,768]{1,0:T(8,128)(2,1)S(1)} %get-tuple-element.39), channel_id=1, source_target_pairs={{0,1},{1,0},{2,3},{3,2},{4,5},{5,4},{6,7},{7,6},{8,9},{9,8},{10,11... | collective-permute-start | bytes 294920 | tf_op jit(solution)/shard_map/ppermute | solution.py:272
  31.8 5.7 %collective-permute-start.1 = (bf16[64,768]{1,0:T(8,128)(2,1)S(1)}, bf16[64,768]{1,0:T(8,128)(2,1)S(1)}, u32[]{:S(2)}, u32[]{:S(2)}) collective-permute-start(bf16[64,768]{1,0:T(8,128)(2,1)S(1)} %get-tuple-element.40), channel_id=1, source_target_pairs={{0,2},{1,3},{2,0},{3,1},{4,6},{5,7},{6,4},{7,5},{8,10},{9,11},{10,... | collective-permute-start | bytes 294920 | tf_op jit(solution)/shard_map/ppermute | solution.py:272
  32.8 6.0 %collective-permute-start.2 = (bf16[64,768]{1,0:T(8,128)(2,1)S(1)}, bf16[64,768]{1,0:T(8,128)(2,1)S(1)}, u32[]{:S(2)}, u32[]{:S(2)}) collective-permute-start(bf16[64,768]{1,0:T(8,128)(2,1)S(1)} %get-tuple-element.41), channel_id=1, source_target_pairs={{0,3},{1,2},{2,1},{3,0},{4,7},{5,6},{6,5},{7,4},{8,11},{9,10},{10,... | collective-permute-start | bytes 294920 | tf_op jit(solution)/shard_map/ppermute | solution.py:272
  33.9 23.8 %collective-permute-start.12 = (bf16[512,256]{1,0:T(8,128)(2,1)S(1)}, bf16[512,256]{1,0:T(8,128)(2,1)S(1)}, u32[]{:S(2)}, u32[]{:S(2)}) collective-permute-start(bf16[512,256]{1,0:T(8,128)(2,1)S(1)} %collective-permute-done.7.refs_10_), channel_id=1, source_target_pairs={{0,8},{4,12},{8,16},{12,20},{16,24},{20,28},{24,0},{28,4},{1,9},{5... | collective-permute-start | bytes 786440 | tf_op jit(solution)/shard_map/ppermute | solution.py:276
  35.7 4.5 %collective-permute-start.3 = (bf16[64,768]{1,0:T(8,128)(2,1)S(1)}, bf16[64,768]{1,0:T(8,128)(2,1)S(1)}, u32[]{:S(2)}, u32[]{:S(2)}) collective-permute-start(bf16[64,768]{1,0:T(8,128)(2,1)S(1)} %get-tuple-element.42), channel_id=1, source_target_pairs={{0,4},{1,5},{2,6},{3,7},{4,0},{5,1},{6,2},{7,3},{8,12},{9,13},{10,... | collective-permute-start | bytes 294920 | tf_op jit(solution)/shard_map/ppermute | solution.py:272
  36.9 5.9 %collective-permute-start.4 = (bf16[64,768]{1,0:T(8,128)(2,1)S(1)}, bf16[64,768]{1,0:T(8,128)(2,1)S(1)}, u32[]{:S(2)}, u32[]{:S(2)}) collective-permute-start(bf16[64,768]{1,0:T(8,128)(2,1)S(1)} %get-tuple-element.43), channel_id=1, source_target_pairs={{0,5},{1,4},{2,7},{3,6},{4,1},{5,0},{6,3},{7,2},{8,13},{9,12},{10,... | collective-permute-start | bytes 294920 | tf_op jit(solution)/shard_map/ppermute | solution.py:272
  37.5 7.5 %collective-permute-start.5 = (bf16[64,768]{1,0:T(8,128)(2,1)S(1)}, bf16[64,768]{1,0:T(8,128)(2,1)S(1)}, u32[]{:S(2)}, u32[]{:S(2)}) collective-permute-start(bf16[64,768]{1,0:T(8,128)(2,1)S(1)} %get-tuple-element.44), channel_id=1, source_target_pairs={{0,6},{1,7},{2,4},{3,5},{4,2},{5,3},{6,0},{7,1},{8,14},{9,15},{10,... | collective-permute-start | bytes 294920 | tf_op jit(solution)/shard_map/ppermute | solution.py:272
  38.8 8.5 %collective-permute-start.6 = (bf16[64,768]{1,0:T(8,128)(2,1)S(1)}, bf16[64,768]{1,0:T(8,128)(2,1)S(1)}, u32[]{:S(2)}, u32[]{:S(2)}) collective-permute-start(bf16[64,768]{1,0:T(8,128)(2,1)S(1)} %get-tuple-element.45), channel_id=1, source_target_pairs={{0,7},{1,6},{2,5},{3,4},{4,3},{5,2},{6,1},{7,0},{8,15},{9,14},{10,... | collective-permute-start | bytes 294920 | tf_op jit(solution)/shard_map/ppermute | solution.py:272
  57.7 1.6 %collective-permute-start.13 = (bf16[512,256]{1,0:T(8,128)(2,1)S(1)}, bf16[512,256]{1,0:T(8,128)(2,1)S(1)}, u32[]{:S(2)}, u32[]{:S(2)}) collective-permute-start(bf16[512,256]{1,0:T(8,128)(2,1)S(1)} %collective-permute-done.12.refs_3_), channel_id=1, source_target_pairs={{0,1},{1,0},{2,3},{3,2},{4,5},{5,4},{6,7},{7,6},{8,9},{9,8},{10,11... | collective-permute-start | bytes 786440 | tf_op jit(solution)/shard_map/ppermute | solution.py:279
  61.7 3.8 %collective-permute-start.14 = (bf16[64,768]{1,0:T(8,128)(2,1)S(1)}, bf16[64,768]{1,0:T(8,128)(2,1)S(1)}, u32[]{:S(2)}, u32[]{:S(2)}) collective-permute-start(bf16[64,768]{1,0:T(8,128)(2,1)S(1)} %get-tuple-element.60), channel_id=1, source_target_pairs={{0,1},{1,0},{2,3},{3,2},{4,5},{5,4},{6,7},{7,6},{8,9},{9,8},{10,11... | collective-permute-start | bytes 294920 | tf_op jit(solution)/shard_map/ppermute | solution.py:272
  62.0 4.9 %collective-permute-start.15 = (bf16[64,768]{1,0:T(8,128)(2,1)S(1)}, bf16[64,768]{1,0:T(8,128)(2,1)S(1)}, u32[]{:S(2)}, u32[]{:S(2)}) collective-permute-start(bf16[64,768]{1,0:T(8,128)(2,1)S(1)} %get-tuple-element.61), channel_id=1, source_target_pairs={{0,2},{1,3},{2,0},{3,1},{4,6},{5,7},{6,4},{7,5},{8,10},{9,11},{10,... | collective-permute-start | bytes 294920 | tf_op jit(solution)/shard_map/ppermute | solution.py:272
  62.5 6.7 %collective-permute-start.16 = (bf16[64,768]{1,0:T(8,128)(2,1)S(1)}, bf16[64,768]{1,0:T(8,128)(2,1)S(1)}, u32[]{:S(2)}, u32[]{:S(2)}) collective-permute-start(bf16[64,768]{1,0:T(8,128)(2,1)S(1)} %get-tuple-element.62), channel_id=1, source_target_pairs={{0,3},{1,2},{2,1},{3,0},{4,7},{5,6},{6,5},{7,4},{8,11},{9,10},{10,... | collective-permute-start | bytes 294920 | tf_op jit(solution)/shard_map/ppermute | solution.py:272
  63.9 5.3 %collective-permute-start.17 = (bf16[64,768]{1,0:T(8,128)(2,1)S(1)}, bf16[64,768]{1,0:T(8,128)(2,1)S(1)}, u32[]{:S(2)}, u32[]{:S(2)}) collective-permute-start(bf16[64,768]{1,0:T(8,128)(2,1)S(1)} %get-tuple-element.63), channel_id=1, source_target_pairs={{0,4},{1,5},{2,6},{3,7},{4,0},{5,1},{6,2},{7,3},{8,12},{9,13},{10,... | collective-permute-start | bytes 294920 | tf_op jit(solution)/shard_map/ppermute | solution.py:272
  64.5 6.4 %collective-permute-start.18 = (bf16[64,768]{1,0:T(8,128)(2,1)S(1)}, bf16[64,768]{1,0:T(8,128)(2,1)S(1)}, u32[]{:S(2)}, u32[]{:S(2)}) collective-permute-start(bf16[64,768]{1,0:T(8,128)(2,1)S(1)} %get-tuple-element.64), channel_id=1, source_target_pairs={{0,5},{1,4},{2,7},{3,6},{4,1},{5,0},{6,3},{7,2},{8,13},{9,12},{10,... | collective-permute-start | bytes 294920 | tf_op jit(solution)/shard_map/ppermute | solution.py:272
  65.5 7.4 %collective-permute-start.19 = (bf16[64,768]{1,0:T(8,128)(2,1)S(1)}, bf16[64,768]{1,0:T(8,128)(2,1)S(1)}, u32[]{:S(2)}, u32[]{:S(2)}) collective-permute-start(bf16[64,768]{1,0:T(8,128)(2,1)S(1)} %get-tuple-element.65), channel_id=1, source_target_pairs={{0,6},{1,7},{2,4},{3,5},{4,2},{5,3},{6,0},{7,1},{8,14},{9,15},{10,... | collective-permute-start | bytes 294920 | tf_op jit(solution)/shard_map/ppermute | solution.py:272
  66.9 8.1 %collective-permute-start.20 = (bf16[64,768]{1,0:T(8,128)(2,1)S(1)}, bf16[64,768]{1,0:T(8,128)(2,1)S(1)}, u32[]{:S(2)}, u32[]{:S(2)}) collective-permute-start(bf16[64,768]{1,0:T(8,128)(2,1)S(1)} %get-tuple-element.66), channel_id=1, source_target_pairs={{0,7},{1,6},{2,5},{3,4},{4,3},{5,2},{6,1},{7,0},{8,15},{9,14},{10,... | collective-permute-start | bytes 294920 | tf_op jit(solution)/shard_map/ppermute | solution.py:272
